TPU v7x, 128 devices: a whole 4x4x4 slice. The times are simulated.
128 devices in a mesh: leaf: 16 (over z, y), clus: 8 (over x, core).
Axes of the slice: x: 4, y: 4, z: 4, core: 2. Of those that a mesh axis runs over, the one named last changes fastest.
Arguments:
- points: bfloat16 [64, 1048576], P(None, ('leaf', 'clus')), may hold values from -6 to 6
- right_side: float32 [8, 1048576], P(None, ('leaf', 'clus')), may hold values from -18 to 18
- near_list: int32 [2048, 8], P(('leaf', 'clus')), may hold values from 0 to 2047, as said below
- near_count: int32 [2048], P(('leaf', 'clus')), may hold values from 3 to 8, as said below
- leaf_skeleton_basis: float32 [2048, 256, 512], P(('leaf', 'clus')), may hold values from -0.25 to 0.25
- leaf_transfer: float32 [2048, 256, 256], P(('leaf', 'clus')), may hold values from -0.375 to 0.375
- pair_transfer: float32 [128, 128, 256], P(('leaf', 'clus')), may hold values from -0.375 to 0.375
- group_transfer: float32 [16, 256, 256], P('leaf'), may hold values from -0.375 to 0.375
- pair_coupling: float32 [128, 4, 256, 128], P(('leaf', 'clus')), may hold values from -0.03125 to 0.03125
- group_coupling: float32 [16, 4, 256, 256], P('leaf'), may hold values from -0.015625 to 0.015625
- top_coupling: float32 [4, 4, 256, 256], replicated, may hold values from -0.0078125 to 0.0078125
- pair_far: int32 [64, 4], replicated, may hold values from 0 to 63
- group_far: int32 [16, 4], P('leaf'), may hold values from 0 to 15
- top_far: int32 [4, 4], replicated, may hold values from 0 to 3
Outputs:
- solution_field: float32 [8, 1048576], P(None, ('leaf', 'clus'))
- residual: float32 [8, 1048576], P(None, ('leaf', 'clus'))
Inputs may be any that keep to these rules, and one draw needn't show every extreme that they name: `near_list`: slot 0 of leaf l is l itself, slot 1 is l - 16 and slot 2 is l + 16, each clipped to the range of leaves; every listed leaf lies among the leaves of the device that holds l and of the devices just before and after it in the order of leaf+clus (leaf index times 8 plus clus index), that is within 16 leaves of l. Slots at or beyond near_count hold valid leaves that are not used. `near_count`: some leaves use all 8 slots.
All inputs are finite; a program needn't handle non-finite values.
Results may differ from a plain program's by a relative error of at most 0.0003.
Values may be sent and summed in bfloat16 or wider, within the bound.
No kernel may reach another device: no remote copies, remote signals or barrier semaphores. Data moves between devices by JAX's collectives and lax.ppermute only.
A program may use at most 128 MiB of HBM per device.

v0:
```python
import functools
import math

import jax
import jax.numpy as jnp
from jax import lax
from jax.experimental import pallas as pl
from jax.experimental.pallas import tpu as pltpu
from jax.sharding import PartitionSpec as P

LEAF = 512
NEAR = 8
FEAT = 64
GROUP = 4
STEP = 4

RIDGE = 1.0
NEAR_SCALE = 1.0 / math.sqrt(NEAR * LEAF)
f32 = jnp.float32
bf16 = jnp.bfloat16
BOTH = ("leaf", "clus")

VMEM = pl.BlockSpec(memory_space=pltpu.VMEM)
SMEM = pl.BlockSpec(memory_space=pltpu.SMEM)
ANY = pl.BlockSpec(memory_space=pl.ANY)


def params(mib=48):
    return pltpu.CompilerParams(vmem_limit_bytes=mib * 2**20)


def split(value):
    high = value.astype(bf16)
    return high, (value - high.astype(f32)).astype(bf16)


def stacked(value):
    high = value.astype(bf16).astype(f32)
    return jnp.concatenate([high, value - high], axis=0).astype(bf16)


def dot_wide(rows, matrix, transposed=False):
    both = stacked(rows)
    count = rows.shape[0]
    dims = (((1,), (1 if transposed else 0,)), ((), ()))
    total = None
    for part in split(matrix):
        out = lax.dot_general(both, part, dims, preferred_element_type=f32)
        out = out[:count] + out[count:]
        total = out if total is None else total + out
    return total


def points_kernel(points, packed, padded, decay):
    leaves = padded.shape[0]
    for leaf in range(leaves):
        block = points[:, leaf * LEAF : (leaf + 1) * LEAF].astype(f32)
        norm = jnp.sum(block * block, axis=0, keepdims=True)
        decay[:, leaf * LEAF : (leaf + 1) * LEAF] = jnp.broadcast_to(
            jnp.exp(norm * (-1.0 / (2.0 * FEAT))), (8, LEAF)
        )
        zero = jnp.zeros((FEAT, LEAF), bf16)
        padded[leaf, 0:FEAT] = zero
        padded[leaf, FEAT : 2 * FEAT] = (block * (1.0 / FEAT)).astype(bf16)
        padded[leaf, 2 * FEAT : 3 * FEAT] = zero
        if leaf % 2 == 1:
            before = points[:, (leaf - 1) * LEAF : leaf * LEAF].astype(f32)
            packed[leaf // 2] = jnp.concatenate([before, block], axis=0).T.astype(bf16)


def prepare_points(points, leaves):
    return pl.pallas_call(
        points_kernel,
        out_shape=[
            jax.ShapeDtypeStruct((leaves // 2, LEAF, 2 * FEAT), bf16),
            jax.ShapeDtypeStruct((leaves, 3 * FEAT, LEAF), bf16),
            jax.ShapeDtypeStruct((8, leaves * LEAF), f32),
        ],
        in_specs=[VMEM],
        out_specs=[VMEM] * 3,
        compiler_params=params(),
        name="prepare_points",
    )(points)


def field_kernel(field, decay, packed, sources):
    lane = lax.broadcasted_iota(jnp.int32, (16, 2 * FEAT), 1)
    for leaf in range(sources.shape[0]):
        columns = slice(leaf * LEAF, (leaf + 1) * LEAF)
        weighted = field[:, columns] * decay[:, columns]
        both = stacked(weighted)
        moments = jnp.dot(both, packed[leaf // 2], preferred_element_type=f32)
        if leaf % 2 == 1:
            moments = pltpu.roll(moments, FEAT, 1)
        total = jnp.sum(both.astype(f32), axis=1, keepdims=True)
        moments = jnp.where(lane < FEAT, moments, jnp.where(lane == FEAT, total, 0.0))
        sources[leaf, :, 0:LEAF] = both
        sources[leaf, :, LEAF : LEAF + 2 * FEAT] = stacked(moments[:8] + moments[8:])


def prepare_field(field, decay, packed, leaves):
    return pl.pallas_call(
        field_kernel,
        out_shape=jax.ShapeDtypeStruct((leaves, 16, LEAF + 2 * FEAT), bf16),
        in_specs=[VMEM] * 3,
        out_specs=VMEM,
        compiler_params=params(),
        name="prepare_field",
    )(field, decay, packed)


def add_pairs(count, pairs, padded, packed, sources, near, moments):
    leaves = padded.shape[0]

    def body(step, carry):
        parts = []
        for unit in range(GROUP):
            code = pairs[step * GROUP + unit]
            target, source = code // 64, code % 64
            start = pl.multiple_of(FEAT * (1 - source % 2), FEAT)
            own = padded[jnp.minimum(target, leaves - 1), pl.ds(start, 2 * FEAT), :]
            gram = jnp.dot(packed[source // 2], own, preferred_element_type=f32)
            rest = (jnp.exp(gram) - (gram + 1.0)).astype(bf16)
            parts.append((target, source, rest))
        for target, source, rest in parts:
            near[target] += jnp.dot(sources[source, :, 0:LEAF], rest, preferred_element_type=f32)
            moments[target] += sources[source, :, LEAF : LEAF + 2 * FEAT].astype(f32)
        return carry

    lax.fori_loop(0, (count + GROUP - 1) // GROUP, body, 0)


def near_inside_kernel(
    count, pairs, padded, packed_own, packed_peer, sources_own, sources_peer,
    near, moments, packed, sources, sems,
):
    leaves = padded.shape[0]
    copies = [
        pltpu.make_async_copy(packed_own, packed.at[pl.ds(0, leaves // 2)], sems.at[0]),
        pltpu.make_async_copy(packed_peer, packed.at[pl.ds(leaves // 2, leaves // 2)], sems.at[1]),
        pltpu.make_async_copy(sources_own, sources.at[pl.ds(0, leaves)], sems.at[2]),
        pltpu.make_async_copy(sources_peer, sources.at[pl.ds(leaves, leaves)], sems.at[3]),
    ]
    for copy in copies:
        copy.start()
    near[...] = jnp.zeros_like(near)
    moments[...] = jnp.zeros_like(moments)
    for copy in copies:
        copy.wait()
    add_pairs(count[0], pairs, padded, packed, sources, near, moments)


def pair_cost(pairs):
    return pl.CostEstimate(
        flops=pairs * 4 * LEAF * LEAF * 256, bytes_accessed=2**23, transcendentals=pairs * LEAF * LEAF
    )


def near_inside(count, pairs, padded, packed_own, packed_peer, sources_own, sources_peer):
    leaves = padded.shape[0]
    width = LEAF + 2 * FEAT
    return pl.pallas_call(
        near_inside_kernel,
        out_shape=[
            jax.ShapeDtypeStruct((leaves + 1, 16, LEAF), f32),
            jax.ShapeDtypeStruct((leaves + 1, 16, 2 * FEAT), f32),
        ],
        in_specs=[SMEM, SMEM, VMEM] + [ANY] * 4,
        out_specs=[VMEM] * 2,
        scratch_shapes=[
            pltpu.VMEM((leaves, LEAF, 2 * FEAT), bf16),
            pltpu.VMEM((2 * leaves, 16, width), bf16),
            pltpu.SemaphoreType.DMA((4,)),
        ],
        compiler_params=params(),
        cost_estimate=pair_cost(56),
        name="near_inside",
    )(count, pairs, padded, packed_own, packed_peer, sources_own, sources_peer)


def near_outside_kernel(
    count, pairs, padded, packed, sources, near_in, moments_in, decay, field, out, near, moments
):
    leaves = padded.shape[0]
    near[...] = near_in[...]
    moments[...] = moments_in[...]
    add_pairs(count[0], pairs, padded, packed, sources, near, moments)
    row = lax.broadcasted_iota(jnp.int32, (2 * FEAT, LEAF), 0)
    for leaf in range(leaves):
        columns = slice(leaf * LEAF, (leaf + 1) * LEAF)
        own = padded[leaf, FEAT : 3 * FEAT, :].astype(f32)
        own = jnp.where(row == FEAT, 1.0, own).astype(bf16)
        sums = moments[leaf]
        smooth = jnp.dot(stacked(sums[:8] + sums[8:]), own, preferred_element_type=f32)
        total = near[leaf] + smooth
        total = (total[:8] + total[8:]) * decay[:, columns]
        out[:, columns] = (total - field[:, columns]) * NEAR_SCALE


def near_outside(count, pairs, padded, packed, sources, near, moments, decay, field):
    leaves = padded.shape[0]
    return pl.pallas_call(
        near_outside_kernel,
        out_shape=jax.ShapeDtypeStruct(field.shape, f32),
        in_specs=[SMEM, SMEM] + [VMEM] * 7,
        out_specs=VMEM,
        scratch_shapes=[
            pltpu.VMEM((leaves + 1, 16, LEAF), f32),
            pltpu.VMEM((leaves + 1, 16, 2 * FEAT), f32),
        ],
        compiler_params=params(),
        cost_estimate=pair_cost(24),
        name="near_outside",
    )(count, pairs, padded, packed, sources, near, moments, decay, field)


def pair_list(mask, codes, empty):
    mask = mask.reshape(-1)
    codes = codes.reshape(-1)
    size = codes.shape[0]
    place = jnp.cumsum(mask.astype(jnp.int32)) - 1
    hits = (place[None, :] == jnp.arange(size, dtype=jnp.int32)[:, None]) & mask[None, :]
    listed = jnp.sum(jnp.where(hits, codes[None, :] - empty, 0), axis=1) + empty
    return jnp.sum(mask.astype(jnp.int32)).reshape(1), listed


def up_kernel(field, basis, transfer, out):
    @pl.when(pl.program_id(0) == 0)
    def _():
        out[...] = jnp.zeros_like(out)

    skeletons = [
        dot_wide(field[:, u * LEAF : (u + 1) * LEAF], basis[u], True) for u in range(STEP)
    ]
    out[...] += sum(dot_wide(skeletons[u], transfer[u]) for u in range(STEP))


def leaf_specs(rank):
    field = pl.BlockSpec((8, STEP * LEAF), lambda i: (0, i))
    basis = pl.BlockSpec((STEP, rank, LEAF), lambda i: (i, 0, 0))
    transfer = pl.BlockSpec((STEP, rank, rank), lambda i: (i, 0, 0))
    return field, basis, transfer


def far_up(field, basis, transfer):
    leaves, rank, _ = basis.shape
    specs = leaf_specs(rank)
    return pl.pallas_call(
        up_kernel,
        out_shape=jax.ShapeDtypeStruct((8, rank), f32),
        grid=(leaves // STEP,),
        in_specs=list(specs),
        out_specs=pl.BlockSpec((8, rank), lambda i: (0, 0)),
        compiler_params=params(),
        name="far_up",
    )(field, basis, transfer)


def whole_expansion(ints, own, peer):
    even = jnp.concatenate([own[...], peer[...]], axis=1)
    odd = jnp.concatenate([peer[...], own[...]], axis=1)
    return jnp.where(ints[0] == 0, even, odd)


def down_up_kernel(ints, own, peer, near, field, basis, transfer, image, upward, dots):
    @pl.when(pl.program_id(0) == 0)
    def _():
        upward[...] = jnp.zeros_like(upward)
        dots[...] = jnp.zeros_like(dots)

    expansion = whole_expansion(ints, own, peer)
    lower = [dot_wide(expansion, transfer[u], True) for u in range(STEP)]
    images = [
        dot_wide(lower[u], basis[u]) + near[:, u * LEAF : (u + 1) * LEAF] for u in range(STEP)
    ]
    skeletons = [dot_wide(images[u], basis[u], True) for u in range(STEP)]
    upward[...] += sum(dot_wide(skeletons[u], transfer[u]) for u in range(STEP))
    for u in range(STEP):
        columns = slice(u * LEAF, (u + 1) * LEAF)
        image[:, columns] = images[u]
        dots[0] += field[:, columns] * field[:, columns]
        dots[1] += field[:, columns] * images[u]
        dots[2] += images[u] * images[u]


def far_down_up(ints, own, peer, near, field, basis, transfer):
    leaves, rank, _ = basis.shape
    specs = leaf_specs(rank)
    half = pl.BlockSpec((8, rank // 2), lambda i: (0, 0))
    return pl.pallas_call(
        down_up_kernel,
        out_shape=[
            jax.ShapeDtypeStruct(near.shape, f32),
            jax.ShapeDtypeStruct((8, rank), f32),
            jax.ShapeDtypeStruct((3, 8, LEAF), f32),
        ],
        grid=(leaves // STEP,),
        in_specs=[SMEM, half, half, specs[0]] + list(specs),
        out_specs=[
            specs[0],
            pl.BlockSpec((8, rank), lambda i: (0, 0)),
            pl.BlockSpec((3, 8, LEAF), lambda i: (0, 0, 0)),
        ],
        compiler_params=params(),
        name="far_down_up",
    )(ints, own, peer, near, field, basis, transfer)


def down_kernel(ints, own, peer, near, field, first, dots_in, basis, transfer, image, dots, late):
    @pl.when(pl.program_id(0) == 0)
    def _():
        late[...] = jnp.zeros_like(late)

    expansion = whole_expansion(ints, own, peer)
    lower = [dot_wide(expansion, transfer[u], True) for u in range(STEP)]
    images = [
        dot_wide(lower[u], basis[u]) + near[:, u * LEAF : (u + 1) * LEAF] for u in range(STEP)
    ]
    for u in range(STEP):
        columns = slice(u * LEAF, (u + 1) * LEAF)
        image[:, columns] = images[u]
        late[0] += field[:, columns] * images[u]
        late[1] += first[:, columns] * images[u]

    @pl.when(pl.program_id(0) == pl.num_programs(0) - 1)
    def _():
        lane = lax.broadcasted_iota(jnp.int32, (8, 128), 1)
        total = jnp.zeros((8, 128), f32)
        for i in range(5):
            products = dots_in[i] if i < 3 else late[i - 3]
            total = jnp.where(lane == i, jnp.sum(products, axis=1, keepdims=True), total)
        dots[...] = total


def far_down(ints, own, peer, near, field, first, dots, basis, transfer):
    leaves, rank, _ = basis.shape
    specs = leaf_specs(rank)
    half = pl.BlockSpec((8, rank // 2), lambda i: (0, 0))
    return pl.pallas_call(
        down_kernel,
        out_shape=[
            jax.ShapeDtypeStruct(near.shape, f32),
            jax.ShapeDtypeStruct((8, 128), f32),
        ],
        grid=(leaves // STEP,),
        in_specs=[SMEM, half, half, specs[0], specs[0], specs[0]]
        + [pl.BlockSpec((3, 8, LEAF), lambda i: (0, 0, 0))]
        + list(specs[1:]),
        out_specs=[specs[0], pl.BlockSpec((8, 128), lambda i: (0, 0))],
        scratch_shapes=[pltpu.VMEM((2, 8, LEAF), f32)],
        compiler_params=params(),
        name="far_down",
    )(ints, own, peer, near, field, first, dots, basis, transfer)


def cluster_kernel(ints, own, peer, pair_transfer, out):
    rank = own.shape[1]
    half = rank // 2
    whole = own[...] + peer[...]
    mine = jnp.where(ints[0] == 0, whole[:, :half], whole[:, half:])
    out[:, :half] = mine
    out[:, half:] = dot_wide(mine, pair_transfer[...])


def group_kernel(shares, group_transfer, out):
    half = shares.shape[2] // 3
    devices = shares.shape[0]
    for node in range(devices // 2):
        out[node, :, :half] = shares[2 * node, :, :half]
        out[node, :, half:] = shares[2 * node + 1, :, :half]
    group = sum(shares[d, :, half:] for d in range(devices))
    out[devices // 2] = group
    out[devices // 2 + 1] = dot_wide(group, group_transfer[...])


def coarse_kernel(
    ints, fields, pair_transfer, group_transfer, pair_coupling, group_coupling, top_coupling, out
):
    slots = pair_coupling.shape[0]
    nodes = 4
    stride = nodes + 2
    pairs = sum(
        dot_wide(
            fields[stride * (ints[1 + k] // nodes) + ints[1 + k] % nodes], pair_coupling[k]
        )
        for k in range(slots)
    )
    groups = sum(
        dot_wide(fields[stride * ints[1 + slots + k] + nodes], group_coupling[k])
        for k in range(slots)
    )
    tops = 0.0
    for k in range(slots):
        first = nodes * ints[1 + 2 * slots + k]
        source = sum(fields[stride * (first + j) + nodes + 1] for j in range(nodes))
        tops += dot_wide(source, top_coupling[k])
    down = groups + dot_wide(tops, group_transfer[...], True)
    out[...] = pairs + dot_wide(down, pair_transfer[...], True)


def cluster_call(kernel, shape, *args, name):
    specs = [SMEM if a.dtype == jnp.int32 else VMEM for a in args]
    return pl.pallas_call(
        kernel,
        out_shape=jax.ShapeDtypeStruct(shape, f32),
        in_specs=specs,
        out_specs=VMEM,
        compiler_params=params(),
        name=name,
    )(*args)


def last_kernel(sums, field, first, second, solved, residual):
    shift = RIDGE + NEAR_SCALE
    dots = jnp.sum(sums[...], axis=0)
    bb, bh, hh, bg, hg = (dots[:, i : i + 1] for i in range(5))
    ratio = bh / bb
    alpha = bb / (shift * bb + bh)
    rest = hh - ratio * bh
    beta = alpha * alpha * rest / bb
    curve = shift * rest + ratio * (ratio * bh - hh) - ratio * bg + hg
    cross = (ratio * bh - hh) + (ratio * (shift * bb + bh) - shift * bh - bg)
    curving = alpha * alpha * curve + alpha * beta * cross + beta * beta * (shift * bb + bh)
    step = alpha * alpha * rest / curving
    gain = alpha * ratio + beta
    b, h, g = field[...], first[...], second[...]
    direction = gain * b - alpha * h
    residue = alpha * (ratio * b - h)
    image = gain * (shift * b + h) - alpha * (shift * h + g)
    solved[...] = alpha * b + step * direction
    residual[...] = residue - step * image


def on_device(
    points,
    right_side,
    near_list,
    near_count,
    leaf_skeleton_basis,
    leaf_transfer,
    pair_transfer,
    group_transfer,
    pair_coupling,
    group_coupling,
    top_coupling,
    pair_far,
    group_far,
    top_far,
):
    leaves = near_list.shape[0]
    device = lax.axis_index(BOTH)
    total = lax.axis_size(BOTH)
    side = device % 2
    node = device // 2
    top_id = lax.axis_index("leaf") // 4
    rank = leaf_skeleton_basis.shape[1]

    swap_in = [(i, i ^ 1) for i in range(total)]
    swap_out = [(i, i + 1) for i in range(1, total - 1, 2)]
    swap_out += [(j, i) for i, j in swap_out]
    inside = lambda value: lax.ppermute(value, BOTH, swap_in)
    outside = lambda value: lax.ppermute(value, BOTH, swap_out)

    ints = jnp.concatenate(
        [
            side.reshape(1),
            lax.dynamic_index_in_dim(pair_far, node, 0, keepdims=False),
            group_far[0],
            lax.dynamic_index_in_dim(top_far, top_id, 0, keepdims=False),
        ]
    ).astype(jnp.int32)
    top_own = lax.dynamic_index_in_dim(top_coupling, top_id, 0, keepdims=False)

    holder = near_list // leaves
    used = jnp.arange(NEAR, dtype=jnp.int32)[None, :] < near_count[:, None]
    target = jnp.broadcast_to(jnp.arange(leaves, dtype=jnp.int32)[:, None], near_list.shape)
    empty = 64 * leaves
    local = holder == device
    peer = holder == (device ^ 1)
    code = 64 * target + near_list % leaves
    count_in, pairs_in = pair_list(
        used & (local | peer), code + jnp.where(peer, leaves, 0), empty
    )
    count_out, pairs_out = pair_list(used & ~(local | peer), code, empty)

    def exchange(partial):
        mine = cluster_call(
            cluster_kernel, (8, 3 * rank // 2), ints, partial, inside(partial), pair_transfer[0],
            name="cluster",
        )
        shares = lax.all_gather(mine, "clus", axis=0)
        block = cluster_call(
            group_kernel, (shares.shape[0] // 2 + 2, 8, rank), shares, group_transfer[0],
            name="group",
        )
        fields = lax.all_gather(block, "leaf", axis=0, tiled=True)
        return cluster_call(
            coarse_kernel, (8, rank // 2), ints, fields, pair_transfer[0], group_transfer[0],
            pair_coupling[0], group_coupling[0], top_own, name="coarse",
        )

    upward = far_up(right_side, leaf_skeleton_basis, leaf_transfer)
    packed, padded, decay = prepare_points(points, leaves)
    packed_peer = inside(packed)
    packed_out = outside(packed)

    def near_field(field):
        sources = prepare_field(field, decay, packed, leaves)
        near, moments = near_inside(
            count_in, pairs_in, padded, packed, packed_peer, sources, inside(sources)
        )
        return near_outside(
            count_out, pairs_out, padded, packed_out, outside(sources), near, moments, decay, field
        )

    down = exchange(upward)
    near = near_field(right_side)
    first, upward, dots = far_down_up(
        ints, down, inside(down), near, right_side, leaf_skeleton_basis, leaf_transfer
    )
    down = exchange(upward)
    near = near_field(first)
    second, dots = far_down(
        ints, down, inside(down), near, right_side, first, dots, leaf_skeleton_basis, leaf_transfer
    )
    sums = lax.all_to_all(jnp.broadcast_to(dots[None, :, :8], (total, 8, 8)), BOTH, 0, 0, tiled=True)
    return pl.pallas_call(
        last_kernel,
        out_shape=[jax.ShapeDtypeStruct(right_side.shape, f32)] * 2,
        in_specs=[VMEM] * 4,
        out_specs=[VMEM] * 2,
        compiler_params=params(),
        name="last",
    )(sums, right_side, first, second)


def solution(mesh):
    in_specs = (
        P(None, BOTH),
        P(None, BOTH),
        P(BOTH, None),
        P(BOTH),
        P(BOTH, None, None),
        P(BOTH, None, None),
        P(BOTH, None, None),
        P("leaf", None, None),
        P(BOTH, None, None, None),
        P("leaf", None, None, None),
        P(),
        P(),
        P("leaf", None),
        P(),
    )
    out_specs = (P(None, BOTH), P(None, BOTH))
    return jax.shard_map(
        on_device, mesh=mesh, in_specs=in_specs, out_specs=out_specs, check_vma=False
    )
```

profile of v0, /device:TPU:1, one launch (start us, length us, event | category | flops | bytes accessed | tf_op | source)
XLA Modules:
  0.0 216.7 jit_solution(9346389706863878977)
XLA Ops:
  0.7 1.2 copy-done.9
  2.5 1.6 copy-done.10
  4.2 1.4 collective-permute-start.4
  5.6 0.9 copy-done.3
  6.6 1.2 prepare_field.2.sources_own
  7.8 3.6 %collective-permute-start.3 = (bf16[16,16,640]{2,1,0:T(8,128)(2,1)}, bf16[16,16,640]{2,1,0:T(8,128)(2,1)}, u32[]{:S(2)}, u32[]{:S(2)}) collective-permute-start(bf16[16,16,640]{2,1,0:T(8,128)(2,1)} %prepare_field.2.sources_own), channel_id=1, source_target_pairs={{1,2},{3,4},{5,6},{7,8},{9,10},{11,12},{13,14},{15,16},{17,18},{19... | collective-permute-start | bytes 983048 | tf_op jit(solution)/shard_map/ppermute | solution.py:462
  11.4 2.0 collective-permute-start.2
  13.4 2.2 %copy-done.1 = f32[16,256,256]{2,1,0:T(8,128)S(1)} copy-done((f32[16,256,256]{2,1,0:T(8,128)S(1)}, f32[16,256,256]{2,1,0:T(8,128)}, u32[]{:S(2)}) %copy-start.1) | copy-done | bytes 4194328
  15.5 5.8 %far_up.1.own = f32[8,256]{1,0:T(8,128)S(1)} custom-call(f32[8,8192]{1,0:T(8,128)S(1)} %copy-done.3, f32[16,256,512]{2,1,0:T(8,128)} %basis.5, f32[16,256,256]{2,1,0:T(8,128)S(1)} %copy-done.1), custom_call_target="tpu_custom_call" | custom-call | tf_op jit(solution)/shard_map/far_up/pallas_call | solution.py:248
  21.6 0.7 convert_reduce_fusion
  24.9 1.3 dynamic-slice_bitcast_fusion.top_coupling
  26.4 0.7 cluster.2
  27.0 14.8 %all-gather = f32[64,384]{1,0:T(8,128)S(1)} all-gather(f32[8,384]{1,0:T(8,128)S(1)} %cluster.2), channel_id=2, replica_groups=mesh['leaf'=16,'clus'=8] {'clus'}, dimensions={0}, use_global_device_ids=true | all-gather | bytes 110592 | tf_op jit(solution)/shard_map/all_gather | solution.py:491
  42.0 23.4 %all_gather.20.fields = f32[96,8,256]{2,1,0:T(8,128)S(1)} all-gather(f32[6,8,256]{2,1,0:T(8,128)S(1)} %group.2), channel_id=1, replica_groups=mesh['leaf'=16,'clus'=8] {'leaf'}, dimensions={0}, use_global_device_ids=true | all-gather | bytes 835584 | tf_op jit(solution)/shard_map/all_gather | solution.py:496
  65.5 1.2 coarse.2.own
  66.7 4.6 %collective-permute-start.1 = (f32[8,128]{1,0:T(8,128)S(1)}, f32[8,128]{1,0:T(8,128)S(1)}, u32[]{:S(2)}, u32[]{:S(2)}) collective-permute-start(f32[8,128]{1,0:T(8,128)S(1)} %coarse.2.own), channel_id=1, source_target_pairs={{0,1},{1,0},{2,3},{3,2},{4,5},{5,4},{6,7},{7,6},{8,9},{9,8},{10,11... | collective-permute-start | bytes 12296 | tf_op jit(solution)/shard_map/ppermute | solution.py:461
  71.3 16.8 %near_inside.2 = (f32[17,16,512]{2,1,0:T(8,128)S(1)}, f32[17,16,128]{2,1,0:T(8,128)S(1)}) custom-call(s32[1]{0:T(128)} %bitcast.10.count, s32[128]{0:T(128)S(1)} %broadcast_add_fusion.1.pairs, bf16[16,192,512]{2,1,0:T(8,128)(2,1)} %copy-done.10, bf16[8,512,128]{2,1,0:T(8,128)(2,1)S(1)} %get-tuple-element.15.packed.packed_own, ...), custom_call_target="tpu_custom_call" | custom-call | flops 15032385536 | bytes 8388608 | tf_op jit(solution)/shard_map/near_inside/pallas_call | solution.py:162
  88.2 1.9 copy-done.11
  90.1 7.3 %near_outside.2.near = f32[8,8192]{1,0:T(8,128)S(1)} custom-call(s32[1]{0:T(128)} %bitcast.9.count, s32[128]{0:T(128)S(1)} %broadcast_add_fusion.2.pairs, bf16[16,192,512]{2,1,0:T(8,128)(2,1)S(1)} %copy-done.11, bf16[8,512,128]{2,1,0:T(8,128)(2,1)} %collective-permute-done.2.packed, bf16[16,16,640]{2,1,0:T(8,128)(2,1)} %collective-permute-done.3.sources, ...), custom_call_target="tpu_custom_call" | custom-call | flops 6442450944 | bytes 8388608 | tf_op jit(solution)/shard_map/near_outside/pallas_call | solution.py:202
  97.4 7.5 %far_down_up.1 = (f32[8,8192]{1,0:T(8,128)S(1)}, f32[8,256]{1,0:T(8,128)S(1)}, f32[3,8,512]{2,1,0:T(8,128)S(1)}) custom-call(s32[13]{0:T(128)S(1)} %pad_add_fusion.ints, f32[8,128]{1,0:T(8,128)S(1)} %coarse.2.own, f32[8,128]{1,0:T(8,128)S(1)} %collective-permute-done.1.peer, f32[8,8192]{1,0:T(8,128)S(1)} %near_outside.2.near, f32[8,8192]{1,0:T(8,128)S(1)} %copy-done.4, ...), custom_call_target="tpu_custom_call" | custom-call | tf_op jit(solution)/shard_map/far_down_up/pallas_call | solution.py:290
  105.3 10.5 %collective-permute-start.9 = (bf16[16,16,640]{2,1,0:T(8,128)(2,1)S(1)}, bf16[16,16,640]{2,1,0:T(8,128)(2,1)S(1)}, u32[]{:S(2)}, u32[]{:S(2)}) collective-permute-start(bf16[16,16,640]{2,1,0:T(8,128)(2,1)S(1)} %prepare_field.3.sources_own), channel_id=1, source_target_pairs={{0,1},{1,0},{2,3},{3,2},{4,5},{5,4},{6,7},{7,6},{8,9},{9,8},{10,11... | collective-permute-start | bytes 983048 | tf_op jit(solution)/shard_map/ppermute | solution.py:461
  115.9 1.9 collective-permute-start.8
  118.5 13.7 %all-gather.1 = f32[64,384]{1,0:T(8,128)S(1)} all-gather(f32[8,384]{1,0:T(8,128)S(1)} %cluster.3), channel_id=3, replica_groups=mesh['leaf'=16,'clus'=8] {'clus'}, dimensions={0}, use_global_device_ids=true | all-gather | bytes 110592 | tf_op jit(solution)/shard_map/all_gather | solution.py:491
  132.4 17.3 %all_gather.23.fields = f32[96,8,256]{2,1,0:T(8,128)S(1)} all-gather(f32[6,8,256]{2,1,0:T(8,128)S(1)} %group.3), channel_id=1, replica_groups=mesh['leaf'=16,'clus'=8] {'leaf'}, dimensions={0}, use_global_device_ids=true | all-gather | bytes 835584 | tf_op jit(solution)/shard_map/all_gather | solution.py:496
  149.6 1.2 coarse.3.own
  150.9 5.6 %collective-permute-start.7 = (f32[8,128]{1,0:T(8,128)S(1)}, f32[8,128]{1,0:T(8,128)S(1)}, u32[]{:S(2)}, u32[]{:S(2)}) collective-permute-start(f32[8,128]{1,0:T(8,128)S(1)} %coarse.3.own), channel_id=1, source_target_pairs={{0,1},{1,0},{2,3},{3,2},{4,5},{5,4},{6,7},{7,6},{8,9},{9,8},{10,11... | collective-permute-start | bytes 12296 | tf_op jit(solution)/shard_map/ppermute | solution.py:461
  156.5 16.6 %near_inside.3 = (f32[17,16,512]{2,1,0:T(8,128)S(1)}, f32[17,16,128]{2,1,0:T(8,128)S(1)}) custom-call(s32[1]{0:T(128)} %bitcast.10.count, s32[128]{0:T(128)S(1)} %broadcast_add_fusion.1.pairs, bf16[16,192,512]{2,1,0:T(8,128)(2,1)} %copy-done.10, bf16[8,512,128]{2,1,0:T(8,128)(2,1)S(1)} %get-tuple-element.15.packed.packed_own, ...), custom_call_target="tpu_custom_call" | custom-call | flops 15032385536 | bytes 8388608 | tf_op jit(solution)/shard_map/near_inside/pallas_call | solution.py:162
  173.1 1.9 copy-done.12
  175.0 6.9 %near_outside.3.near = f32[8,8192]{1,0:T(8,128)S(1)} custom-call(s32[1]{0:T(128)} %bitcast.9.count, s32[128]{0:T(128)S(1)} %broadcast_add_fusion.2.pairs, bf16[16,192,512]{2,1,0:T(8,128)(2,1)S(1)} %copy-done.12, bf16[8,512,128]{2,1,0:T(8,128)(2,1)} %collective-permute-done.2.packed, bf16[16,16,640]{2,1,0:T(8,128)(2,1)S(1)} %collective-permute-done.8.sources, ...), custom_call_target="tpu_custom_call" | custom-call | flops 6442450944 | bytes 8388608 | tf_op jit(solution)/shard_map/near_outside/pallas_call | solution.py:202
  181.9 5.6 %far_down.1 = (f32[8,8192]{1,0:T(8,128)S(1)}, f32[8,128]{1,0:T(8,128)S(1)}) custom-call(s32[13]{0:T(128)S(1)} %pad_add_fusion.ints, f32[8,128]{1,0:T(8,128)S(1)} %coarse.3.own, f32[8,128]{1,0:T(8,128)S(1)} %collective-permute-done.7.peer, f32[8,8192]{1,0:T(8,128)S(1)} %near_outside.3.near, f32[8,8192]{1,0:T(8,128)S(1)} %copy-done.4, ...), custom_call_target="tpu_custom_call" | custom-call | tf_op jit(solution)/shard_map/far_down/pallas_call | solution.py:339
  187.6 27.7 %all_to_all.5.sums = f32[128,8,8]{2,1,0:T(8,128)S(1)} all-to-all(f32[128,8,8]{2,1,0:T(8,128)S(1)} %broadcast_in_dim.44), channel_id=1, replica_groups=mesh['leaf'=16,'clus'=8] {'leaf','clus'}, dimensions={0} | all-to-all | bytes 65536 | tf_op jit(solution)/shard_map/all_to_all | solution.py:526
  215.4 1.4 last.1
  (75 shorter events, 5.1 us)
Async XLA Ops:
  0.6 23.6 %copy-start = (s32[4,4]{1,0:T(4,128)S(1)}, s32[4,4]{1,0:T(4,128)}, u32[]{:S(2)}) copy-start(s32[4,4]{1,0:T(4,128)} %param.27) | copy-start | bytes 196
  0.6 1.2 copy-start.9
  2.5 1.6 copy-start.10
  4.2 67.1 %collective-permute-start.4 = (bf16[8,512,128]{2,1,0:T(8,128)(2,1)S(1)}, bf16[8,512,128]{2,1,0:T(8,128)(2,1)}, u32[]{:S(2)}, u32[]{:S(2)}) collective-permute-start(bf16[8,512,128]{2,1,0:T(8,128)(2,1)S(1)} %get-tuple-element.15.packed.packed_own), channel_id=1, source_target_pairs={{0,1},{1,0},{2,3},{3,2},{4,5},{5,4},{6,7},{7,6},{8,9},{9,8},{10,11... | collective-permute-start | bytes 3145736 | tf_op jit(solution)/shard_map/ppermute | solution.py:461
  5.6 0.9 copy-start.3
  6.5 14.9 %copy-start.13 = (s32[16,8]{0,1:T(8,128)S(1)}, s32[16,8]{0,1:T(8,128)}, u32[]{:S(2)}) copy-start(s32[16,8]{0,1:T(8,128)} %param.16) | copy-start | bytes 1540
  6.5 14.9 %copy-start.15 = (s32[16]{0:T(128)S(1)}, s32[16]{0:T(128)}, u32[]{:S(2)}) copy-start(s32[16]{0:T(128)} %param.17) | copy-start | bytes 196
  6.5 18.1 %copy-start.14 = (s32[64,4]{0,1:T(4,128)S(1)}, s32[64,4]{0,1:T(4,128)}, u32[]{:S(2)}) copy-start(s32[64,4]{0,1:T(4,128)} %param.25) | copy-start | bytes 3076
  6.5 19.7 %copy-start.16 = (s32[1,4]{1,0:T(1,128)S(1)}, s32[1,4]{1,0:T(1,128)}, u32[]{:S(2)}) copy-start(s32[1,4]{1,0:T(1,128)} %param.26) | copy-start | bytes 52
  6.5 19.8 %copy-start.8 = (f32[1,128,256]{2,1,0:T(8,128)S(1)}, f32[1,128,256]{2,1,0:T(8,128)}, u32[]{:S(2)}) copy-start(f32[1,128,256]{2,1,0:T(8,128)} %param.20) | copy-start | bytes 393220
  6.6 35.3 %copy-start.6 = (f32[1,256,256]{2,1,0:T(8,128)S(1)}, f32[1,256,256]{2,1,0:T(8,128)}, u32[]{:S(2)}) copy-start(f32[1,256,256]{2,1,0:T(8,128)} %param.21) | copy-start | bytes 786436
  7.8 63.5 %collective-permute-start.5 = (bf16[16,16,640]{2,1,0:T(8,128)(2,1)}, bf16[16,16,640]{2,1,0:T(8,128)(2,1)}, u32[]{:S(2)}, u32[]{:S(2)}) collective-permute-start(bf16[16,16,640]{2,1,0:T(8,128)(2,1)} %prepare_field.2.sources_own), channel_id=1, source_target_pairs={{0,1},{1,0},{2,3},{3,2},{4,5},{5,4},{6,7},{7,6},{8,9},{9,8},{10,11... | collective-permute-start | bytes 983048 | tf_op jit(solution)/shard_map/ppermute | solution.py:461
  7.8 80.4 %collective-permute-start.3 = (bf16[16,16,640]{2,1,0:T(8,128)(2,1)}, bf16[16,16,640]{2,1,0:T(8,128)(2,1)}, u32[]{:S(2)}, u32[]{:S(2)}) collective-permute-start(bf16[16,16,640]{2,1,0:T(8,128)(2,1)} %prepare_field.2.sources_own), channel_id=1, source_target_pairs={{1,2},{3,4},{5,6},{7,8},{9,10},{11,12},{13,14},{15,16},{17,18},{19... | collective-permute-start | bytes 983048 | tf_op jit(solution)/shard_map/ppermute | solution.py:462
  11.4 76.8 %collective-permute-start.2 = (bf16[8,512,128]{2,1,0:T(8,128)(2,1)S(1)}, bf16[8,512,128]{2,1,0:T(8,128)(2,1)}, u32[]{:S(2)}, u32[]{:S(2)}) collective-permute-start(bf16[8,512,128]{2,1,0:T(8,128)(2,1)S(1)} %get-tuple-element.15.packed.packed_own), channel_id=1, source_target_pairs={{1,2},{3,4},{5,6},{7,8},{9,10},{11,12},{13,14},{15,16},{17,18},{19... | collective-permute-start | bytes 3145736 | tf_op jit(solution)/shard_map/ppermute | solution.py:462
  13.4 2.2 %copy-start.1 = (f32[16,256,256]{2,1,0:T(8,128)S(1)}, f32[16,256,256]{2,1,0:T(8,128)}, u32[]{:S(2)}) copy-start(f32[16,256,256]{2,1,0:T(8,128)} %transfer.5) | copy-start | bytes 12582916
  21.3 44.1 %copy-start.5 = (f32[1,4,256,256]{3,2,1,0:T(8,128)S(1)}, f32[1,4,256,256]{3,2,1,0:T(8,128)}, u32[]{:S(2)}) copy-start(f32[1,4,256,256]{3,2,1,0:T(8,128)} %param.23) | copy-start | bytes 3145732
  21.3 44.1 %copy-start.7 = (f32[1,4,256,128]{3,2,1,0:T(8,128)S(1)}, f32[1,4,256,128]{3,2,1,0:T(8,128)}, u32[]{:S(2)}) copy-start(f32[1,4,256,128]{3,2,1,0:T(8,128)} %param.22) | copy-start | bytes 1572868
  21.3 5.0 %collective-permute-start = (f32[8,256]{1,0:T(8,128)S(1)}, f32[8,256]{1,0:T(8,128)S(1)}, u32[]{:S(2)}, u32[]{:S(2)}) collective-permute-start(f32[8,256]{1,0:T(8,128)S(1)} %far_up.1.own), channel_id=1, source_target_pairs={{0,1},{1,0},{2,3},{3,2},{4,5},{5,4},{6,7},{7,6},{8,9},{9,8},{10,11... | collective-permute-start | bytes 24584 | tf_op jit(solution)/shard_map/ppermute | solution.py:461
  66.7 30.6 %collective-permute-start.1 = (f32[8,128]{1,0:T(8,128)S(1)}, f32[8,128]{1,0:T(8,128)S(1)}, u32[]{:S(2)}, u32[]{:S(2)}) collective-permute-start(f32[8,128]{1,0:T(8,128)S(1)} %coarse.2.own), channel_id=1, source_target_pairs={{0,1},{1,0},{2,3},{3,2},{4,5},{5,4},{6,7},{7,6},{8,9},{9,8},{10,11... | collective-permute-start | bytes 12296 | tf_op jit(solution)/shard_map/ppermute | solution.py:461
  71.3 16.9 %copy-start.4 = (f32[8,8192]{1,0:T(8,128)S(1)}, f32[8,8192]{1,0:T(8,128)}, u32[]{:S(2)}) copy-start(f32[8,8192]{1,0:T(8,128)} %field.11) | copy-start | bytes 786436
  88.2 1.9 copy-start.11
  90.1 7.3 %copy-start.2 = (f32[16,256,256]{2,1,0:T(8,128)S(1)}, f32[16,256,256]{2,1,0:T(8,128)}, u32[]{:S(2)}) copy-start(f32[16,256,256]{2,1,0:T(8,128)} %transfer.5) | copy-start | bytes 12582916
  105.3 51.2 %collective-permute-start.9 = (bf16[16,16,640]{2,1,0:T(8,128)(2,1)S(1)}, bf16[16,16,640]{2,1,0:T(8,128)(2,1)S(1)}, u32[]{:S(2)}, u32[]{:S(2)}) collective-permute-start(bf16[16,16,640]{2,1,0:T(8,128)(2,1)S(1)} %prepare_field.3.sources_own), channel_id=1, source_target_pairs={{0,1},{1,0},{2,3},{3,2},{4,5},{5,4},{6,7},{7,6},{8,9},{9,8},{10,11... | collective-permute-start | bytes 983048 | tf_op jit(solution)/shard_map/ppermute | solution.py:461
  115.8 2.0 collective-permute-start.6
  115.9 57.2 %collective-permute-start.8 = (bf16[16,16,640]{2,1,0:T(8,128)(2,1)S(1)}, bf16[16,16,640]{2,1,0:T(8,128)(2,1)S(1)}, u32[]{:S(2)}, u32[]{:S(2)}) collective-permute-start(bf16[16,16,640]{2,1,0:T(8,128)(2,1)S(1)} %prepare_field.3.sources_own), channel_id=1, source_target_pairs={{1,2},{3,4},{5,6},{7,8},{9,10},{11,12},{13,14},{15,16},{17,18},{19... | collective-permute-start | bytes 983048 | tf_op jit(solution)/shard_map/ppermute | solution.py:462
  150.9 31.1 %collective-permute-start.7 = (f32[8,128]{1,0:T(8,128)S(1)}, f32[8,128]{1,0:T(8,128)S(1)}, u32[]{:S(2)}, u32[]{:S(2)}) collective-permute-start(f32[8,128]{1,0:T(8,128)S(1)} %coarse.3.own), channel_id=1, source_target_pairs={{0,1},{1,0},{2,3},{3,2},{4,5},{5,4},{6,7},{7,6},{8,9},{9,8},{10,11... | collective-permute-start | bytes 12296 | tf_op jit(solution)/shard_map/ppermute | solution.py:461
  173.1 1.9 copy-start.12
where the time goes:
time: 219 us; the launch traced here: 217 us
  blocking collectives  96.9 us (44%)
  Pallas kernels  74.4 us (34%)
  starting transfers between devices  29.8 us (14%)
  local copies, waits for them, and re-layouts  12.3 us (6%)
  other arithmetic  2.25 us (1%)
    all_gather x2, blocking collectives, exchange(): fields = lax.all_gather(block, 'leaf', axis=0, tiled=True)  40.7 us
    pallas_call x2, Pallas kernels, near_inside(): pl.pallas_call(near_inside_kernel, out_shape=[jax.ShapeDtypeStruct((leave...  33.4 us
    all_gather x2, blocking collectives, exchange(): shares = lax.all_gather(mine, 'clus', axis=0)  28.5 us
    all_to_all x1, blocking collectives, on_device(): lax.all_to_all(jnp.broadcast_to(dots[None, :, :8], (total, 8, 8)), BOTH,...  27.7 us
    ppermute x7, starting transfers between devices, on_device(): inside = lambda value: lax.ppermute(value, BOTH, swap_in)  22.3 us
    pallas_call x2, Pallas kernels, near_outside(): pl.pallas_call(near_outside_kernel, out_shape=jax.ShapeDtypeStruct(field....  14.2 us
    unnamed x34, local copies, waits for them, and re-layouts  9.81 us
    pallas_call x1, Pallas kernels, far_down_up(): pl.pallas_call(down_up_kernel, out_shape=[jax.ShapeDtypeStruct(near.shape...  7.51 us
  transfers between devices with their start and end apart: 10, of which 0 were waited for; matrix products, arithmetic and copies ran while one was open for 2% of the time, Pallas kernels for 27%

commit v1 on v0

v1 whole, which is shorter than its diff:
```python
import functools
import math

import jax
import jax.numpy as jnp
from jax import lax
from jax.experimental import pallas as pl
from jax.experimental.pallas import tpu as pltpu
from jax.sharding import PartitionSpec as P

LEAF = 512
NEAR = 8
FEAT = 64
GROUP = 8
SOURCE = 80
STEP = 4

RIDGE = 1.0
LOG2_E = math.log2(math.e)
NEAR_SCALE = 1.0 / math.sqrt(NEAR * LEAF)
f32 = jnp.float32
bf16 = jnp.bfloat16
BOTH = ("leaf", "clus")

VMEM = pl.BlockSpec(memory_space=pltpu.VMEM)
SMEM = pl.BlockSpec(memory_space=pltpu.SMEM)
ANY = pl.BlockSpec(memory_space=pl.ANY)


def params(mib=48):
    return pltpu.CompilerParams(vmem_limit_bytes=mib * 2**20)


def split(value):
    high = value.astype(bf16)
    return high, (value - high.astype(f32)).astype(bf16)


def stacked(value):
    high = value.astype(bf16).astype(f32)
    return jnp.concatenate([high, value - high], axis=0).astype(bf16)


def turned(rows):
    high = rows.astype(bf16).astype(f32)
    return jnp.concatenate([high, rows - high], axis=0).T.astype(bf16)


def dot_turned(matrix, columns):
    high, low = split(matrix)
    out = jnp.dot(high, columns, preferred_element_type=f32)
    out = (out + jnp.dot(low, columns, preferred_element_type=f32)).T
    count = columns.shape[1] // 2
    return out[:count] + out[count:]


def dot_wide(rows, matrix):
    both = stacked(rows)
    high, low = split(matrix)
    out = jnp.dot(both, high, preferred_element_type=f32)
    out += jnp.dot(both, low, preferred_element_type=f32)
    count = rows.shape[0]
    return out[:count] + out[count:]


def halo_kernel(points, field, packed_sources, decay):
    leaves = points.shape[1] // LEAF
    for leaf in range(leaves):
        columns = slice(leaf * LEAF, (leaf + 1) * LEAF)
        block = points[:, columns].astype(f32)
        norm = jnp.sum(block * block, axis=0, keepdims=True)
        decay[:, columns] = jnp.broadcast_to(jnp.exp(norm * (-1.0 / (2.0 * FEAT))), (8, LEAF))
        if leaf % 2 == 1:
            before = points[:, (leaf - 1) * LEAF : leaf * LEAF].astype(f32)
            turned = jnp.concatenate([before, block], axis=0).T.astype(bf16)
            packed_sources[leaf // 2 * LEAF : (leaf // 2 + 1) * LEAF, :] = turned
    start = leaves // 2 * LEAF
    write_sources(field, decay, packed_sources, packed_sources, start, leaves)


def write_sources(field, decay, packed, out, start, leaves):
    lane = lax.broadcasted_iota(jnp.int32, (16, 2 * FEAT), 1)
    for leaf in range(leaves):
        columns = slice(leaf * LEAF, (leaf + 1) * LEAF)
        both = stacked(field[:, columns] * decay[:, columns])
        points = packed[leaf // 2 * LEAF : (leaf // 2 + 1) * LEAF, :]
        moments = jnp.dot(both, points, preferred_element_type=f32)
        if leaf % 2 == 1:
            moments = pltpu.roll(moments, FEAT, 1)
        total = jnp.sum(both.astype(f32), axis=1, keepdims=True)
        moments = jnp.where(lane < FEAT, moments, jnp.where(lane == FEAT, total, 0.0))
        first = start + leaf * SOURCE
        for chunk in range(LEAF // 128):
            out[first + 16 * chunk : first + 16 * (chunk + 1), :] = both[
                :, 128 * chunk : 128 * (chunk + 1)
            ]
        out[first + LEAF // 8 : first + SOURCE, :] = stacked(moments[:8] + moments[8:])


def first_halo(points, field):
    leaves = field.shape[1] // LEAF
    rows = leaves // 2 * LEAF + leaves * SOURCE
    return pl.pallas_call(
        halo_kernel,
        out_shape=[
            jax.ShapeDtypeStruct((rows, 128), bf16),
            jax.ShapeDtypeStruct((8, leaves * LEAF), f32),
        ],
        in_specs=[VMEM] * 2,
        out_specs=[VMEM] * 2,
        compiler_params=params(16),
        name="first_halo",
    )(points, field)


def next_halo_kernel(field, decay, packed, out):
    write_sources(field, decay, packed, out, 0, out.shape[0] // SOURCE)


def next_halo(field, decay, packed):
    leaves = field.shape[1] // LEAF
    whole = lambda shape: pl.BlockSpec(shape, lambda i: (0, 0))
    return pl.pallas_call(
        next_halo_kernel,
        out_shape=jax.ShapeDtypeStruct((leaves * SOURCE, 128), bf16),
        grid=(1,),
        in_specs=[whole(field.shape), whole(decay.shape), whole((leaves // 2 * LEAF, 128))],
        out_specs=whole((leaves * SOURCE, 128)),
        compiler_params=params(16),
        name="next_halo",
    )(field, decay, packed)


def near_kernel(
    count, pairs, points, field, decay, own_points, peer_points, out_points,
    own_sources, peer_sources, out_sources, out, near, moments, padded, packed, sources, sems,
):
    leaves = field.shape[1] // LEAF
    rows = leaves // 2 * LEAF
    copies = []
    for i, ref in enumerate([own_points, peer_points, out_points]):
        copies.append(
            pltpu.make_async_copy(
                ref.at[pl.ds(0, rows)], packed.at[pl.ds(i * rows, rows)], sems.at[i]
            )
        )
    for i, ref in enumerate([own_sources, peer_sources, out_sources]):
        begin = ref.shape[0] - leaves * SOURCE
        copies.append(
            pltpu.make_async_copy(
                ref.at[pl.ds(begin, leaves * SOURCE)],
                sources.at[pl.ds(i * leaves * SOURCE, leaves * SOURCE)],
                sems.at[3 + i],
            )
        )
    for copy in copies:
        copy.start()
    near[...] = jnp.zeros_like(near)
    moments[...] = jnp.zeros_like(moments)
    zero = jnp.zeros((FEAT, LEAF), bf16)
    for leaf in range(leaves):
        block = points[:, leaf * LEAF : (leaf + 1) * LEAF].astype(f32)
        high, low = split(block * (LOG2_E / FEAT))
        for i, part in enumerate([zero, high, zero, low, zero]):
            padded[leaf, i * FEAT : (i + 1) * FEAT] = part
    for copy in copies:
        copy.wait()

    def add_pairs(first, size):
        parts = []
        for unit in range(size):
            code = pairs[first + unit]
            target, source = lax.shift_right_logical(code, 6), code & 63
            start = pl.multiple_of(FEAT * (1 - (source & 1)), FEAT)
            own = padded[jnp.minimum(target, leaves - 1), pl.ds(start, 4 * FEAT), :]
            place = pl.multiple_of(lax.shift_right_logical(source, 1) * LEAF, LEAF)
            other = packed[pl.ds(place, LEAF), :]
            gram = jnp.dot(
                jnp.concatenate([other, other], axis=1), own, preferred_element_type=f32
            )
            parts.append((target, source, (jnp.exp2(gram) - (gram + 1.0)).astype(bf16)))
        for target, source, rest in parts:
            begin = pl.multiple_of(source * SOURCE, SOURCE)
            chunks = [
                sources[pl.ds(pl.multiple_of(begin + 16 * c, 16), 16), :] for c in range(LEAF // 128 + 1)
            ]
            weighted = jnp.concatenate(chunks[:-1], axis=1)
            near[target] += jnp.dot(weighted, rest, preferred_element_type=f32)
            moments[target] += chunks[-1].astype(f32)

    def many(step, carry):
        add_pairs(step * GROUP, GROUP)
        return carry

    def few(step, carry):
        add_pairs(whole * GROUP + 2 * step, 2)
        return carry

    whole = lax.div(count[0], GROUP)
    left = count[0] - whole * GROUP
    lax.fori_loop(0, whole, many, 0)
    lax.fori_loop(0, lax.div(left + 1, 2), few, 0)

    row = lax.broadcasted_iota(jnp.int32, (2 * FEAT, LEAF), 0)
    for leaf in range(leaves):
        columns = slice(leaf * LEAF, (leaf + 1) * LEAF)
        scaled = points[:, columns].astype(f32) * (LOG2_E / FEAT)
        high, low = split(scaled)
        sums = moments[leaf]
        sums = sums[:8] + sums[8:]
        both = stacked(sums)
        total = near[leaf] + jnp.dot(both[:, :FEAT], high, preferred_element_type=f32)
        total += jnp.dot(both[:, :FEAT], low, preferred_element_type=f32)
        total = total[:8] + total[8:] + sums[:, FEAT : FEAT + 1]
        out[:, columns] = (total * decay[:, columns] - field[:, columns]) * NEAR_SCALE


def near_field(count, pairs, points, field, decay, halo, sources):
    leaves = field.shape[1] // LEAF
    pairs_guess = 88
    return pl.pallas_call(
        near_kernel,
        out_shape=jax.ShapeDtypeStruct(field.shape, f32),
        in_specs=[SMEM, SMEM, VMEM, VMEM, VMEM] + [ANY] * 6,
        out_specs=VMEM,
        scratch_shapes=[
            pltpu.VMEM((leaves + 1, 16, LEAF), f32),
            pltpu.VMEM((leaves + 1, 16, 128), f32),
            pltpu.VMEM((leaves, 5 * FEAT, LEAF), bf16),
            pltpu.VMEM((3 * leaves // 2 * LEAF, 128), bf16),
            pltpu.VMEM((3 * leaves * SOURCE, 128), bf16),
            pltpu.SemaphoreType.DMA((6,)),
        ],
        compiler_params=params(44),
        cost_estimate=pl.CostEstimate(
            flops=pairs_guess * 4 * LEAF * LEAF * 256,
            bytes_accessed=2**23,
            transcendentals=pairs_guess * LEAF * LEAF,
        ),
        name="near_field",
    )(count, pairs, points, field, decay, *halo, *sources)


def pair_list(mask, codes, empty):
    mask = mask.reshape(-1)
    codes = codes.reshape(-1)
    size = codes.shape[0]
    place = jnp.cumsum(mask.astype(jnp.int32)) - 1
    hits = (place[None, :] == jnp.arange(size, dtype=jnp.int32)[:, None]) & mask[None, :]
    listed = jnp.sum(jnp.where(hits, codes[None, :] - empty, 0), axis=1) + empty
    return jnp.sum(mask.astype(jnp.int32)).reshape(1), listed


def up_kernel(field, basis, transfer, out):
    @pl.when(pl.program_id(0) == 0)
    def _():
        out[...] = jnp.zeros_like(out)

    skeletons = [
        dot_turned(basis[u], turned(field[:, u * LEAF : (u + 1) * LEAF])) for u in range(STEP)
    ]
    out[...] += sum(dot_wide(skeletons[u], transfer[u]) for u in range(STEP))


def leaf_specs(rank):
    field = pl.BlockSpec((8, STEP * LEAF), lambda i: (0, i))
    basis = pl.BlockSpec((STEP, rank, LEAF), lambda i: (i, 0, 0))
    transfer = pl.BlockSpec((STEP, rank, rank), lambda i: (i, 0, 0))
    return field, basis, transfer


def far_up(field, basis, transfer):
    leaves, rank, _ = basis.shape
    specs = leaf_specs(rank)
    return pl.pallas_call(
        up_kernel,
        out_shape=jax.ShapeDtypeStruct((8, rank), f32),
        grid=(leaves // STEP,),
        in_specs=list(specs),
        out_specs=pl.BlockSpec((8, rank), lambda i: (0, 0)),
        compiler_params=params(),
        name="far_up",
    )(field, basis, transfer)


def whole_expansion(ints, own, peer):
    even = jnp.concatenate([own[...], peer[...]], axis=1)
    odd = jnp.concatenate([peer[...], own[...]], axis=1)
    return jnp.where(ints[0] == 0, even, odd)


def down_up_kernel(ints, own, peer, near, field, basis, transfer, image, upward, dots):
    @pl.when(pl.program_id(0) == 0)
    def _():
        upward[...] = jnp.zeros_like(upward)
        dots[...] = jnp.zeros_like(dots)

    expansion = turned(whole_expansion(ints, own, peer))
    lower = [dot_turned(transfer[u], expansion) for u in range(STEP)]
    images = [
        dot_wide(lower[u], basis[u]) + near[:, u * LEAF : (u + 1) * LEAF] for u in range(STEP)
    ]
    skeletons = [dot_turned(basis[u], turned(images[u])) for u in range(STEP)]
    upward[...] += sum(dot_wide(skeletons[u], transfer[u]) for u in range(STEP))
    for u in range(STEP):
        columns = slice(u * LEAF, (u + 1) * LEAF)
        image[:, columns] = images[u]
        dots[0] += field[:, columns] * field[:, columns]
        dots[1] += field[:, columns] * images[u]
        dots[2] += images[u] * images[u]


def far_down_up(ints, own, peer, near, field, basis, transfer):
    leaves, rank, _ = basis.shape
    specs = leaf_specs(rank)
    half = pl.BlockSpec((8, rank // 2), lambda i: (0, 0))
    return pl.pallas_call(
        down_up_kernel,
        out_shape=[
            jax.ShapeDtypeStruct(near.shape, f32),
            jax.ShapeDtypeStruct((8, rank), f32),
            jax.ShapeDtypeStruct((3, 8, LEAF), f32),
        ],
        grid=(leaves // STEP,),
        in_specs=[SMEM, half, half, specs[0]] + list(specs),
        out_specs=[
            specs[0],
            pl.BlockSpec((8, rank), lambda i: (0, 0)),
            pl.BlockSpec((3, 8, LEAF), lambda i: (0, 0, 0)),
        ],
        compiler_params=params(),
        name="far_down_up",
    )(ints, own, peer, near, field, basis, transfer)


def dot_place():
    lane = lax.broadcasted_iota(jnp.int32, (8, 128), 1)
    row = lax.broadcasted_iota(jnp.int32, (8, 128), 0)
    return jnp.where((lane & 7) == row, lax.shift_right_logical(lane, 3), -1)


def down_kernel(ints, own, peer, near, field, first, dots_in, basis, transfer, image, dots, late):
    @pl.when(pl.program_id(0) == 0)
    def _():
        late[...] = jnp.zeros_like(late)

    expansion = turned(whole_expansion(ints, own, peer))
    lower = [dot_turned(transfer[u], expansion) for u in range(STEP)]
    images = [
        dot_wide(lower[u], basis[u]) + near[:, u * LEAF : (u + 1) * LEAF] for u in range(STEP)
    ]
    for u in range(STEP):
        columns = slice(u * LEAF, (u + 1) * LEAF)
        image[:, columns] = images[u]
        late[0] += field[:, columns] * images[u]
        late[1] += first[:, columns] * images[u]

    @pl.when(pl.program_id(0) == pl.num_programs(0) - 1)
    def _():
        place = dot_place()
        total = jnp.zeros((8, 128), f32)
        for i in range(5):
            products = dots_in[i] if i < 3 else late[i - 3]
            total = jnp.where(place == i, jnp.sum(products, axis=1, keepdims=True), total)
        row = jnp.sum(total, axis=0, keepdims=True)
        dots[...] = jnp.broadcast_to(row[None], dots.shape)


def far_down(ints, own, peer, near, field, first, dots, basis, transfer, devices):
    leaves, rank, _ = basis.shape
    specs = leaf_specs(rank)
    half = pl.BlockSpec((8, rank // 2), lambda i: (0, 0))
    return pl.pallas_call(
        down_kernel,
        out_shape=[
            jax.ShapeDtypeStruct(near.shape, f32),
            jax.ShapeDtypeStruct((devices, 1, 128), f32),
        ],
        grid=(leaves // STEP,),
        in_specs=[SMEM, half, half, specs[0], specs[0], specs[0]]
        + [pl.BlockSpec((3, 8, LEAF), lambda i: (0, 0, 0))]
        + list(specs[1:]),
        out_specs=[specs[0], pl.BlockSpec((devices, 1, 128), lambda i: (0, 0, 0))],
        scratch_shapes=[pltpu.VMEM((2, 8, LEAF), f32)],
        compiler_params=params(),
        name="far_down",
    )(ints, own, peer, near, field, first, dots, basis, transfer)


def cluster_kernel(ints, own, peer, pair_transfer, out):
    rank = own.shape[1]
    half = rank // 2
    whole = own[...] + peer[...]
    mine = jnp.where(ints[0] == 0, whole[:, :half], whole[:, half:])
    share = jnp.concatenate([mine, dot_wide(mine, pair_transfer[...])], axis=1)
    out[...] = jnp.broadcast_to(share[None], out.shape)


def group_kernel(shares, group_transfer, out):
    half = shares.shape[2] // 3
    devices = shares.shape[0]
    group = sum(shares[d, :, half:] for d in range(devices))
    lift = dot_wide(group, group_transfer[...])
    for copy in range(out.shape[0]):
        for node in range(devices // 2):
            out[copy, node, :, :half] = shares[2 * node, :, :half]
            out[copy, node, :, half:] = shares[2 * node + 1, :, :half]
        out[copy, devices // 2] = group
        out[copy, devices // 2 + 1] = lift


def coarse_kernel(
    ints, fields, pair_transfer, group_transfer, pair_coupling, group_coupling, top_coupling,
    out, own_top, sem,
):
    slots = pair_coupling.shape[0]
    copy = pltpu.make_async_copy(top_coupling.at[ints[1 + 3 * slots]], own_top, sem)
    copy.start()
    nodes = 4
    stride = nodes + 2
    pairs = sum(
        dot_wide(
            fields[stride * (ints[1 + k] // nodes) + ints[1 + k] % nodes], pair_coupling[k]
        )
        for k in range(slots)
    )
    groups = sum(
        dot_wide(fields[stride * ints[1 + slots + k] + nodes], group_coupling[k])
        for k in range(slots)
    )
    copy.wait()
    tops = 0.0
    for k in range(slots):
        first = nodes * ints[1 + 2 * slots + k]
        source = sum(fields[stride * (first + j) + nodes + 1] for j in range(nodes))
        tops += dot_wide(source, own_top[k])
    down = groups + dot_turned(group_transfer[...], turned(tops))
    out[...] = pairs + dot_turned(pair_transfer[...], turned(down))


def cluster_call(kernel, shape, *args, name, scratch=(), far_away=()):
    specs = [SMEM if a.dtype == jnp.int32 else VMEM for a in args] + [ANY] * len(far_away)
    return pl.pallas_call(
        kernel,
        out_shape=jax.ShapeDtypeStruct(shape, f32),
        in_specs=specs,
        out_specs=VMEM,
        scratch_shapes=scratch,
        compiler_params=params(16),
        name=name,
    )(*args, *far_away)


def last_kernel(sums, field, first, second, solved, residual):
    shift = RIDGE + NEAR_SCALE
    dots = jnp.broadcast_to(jnp.sum(sums[...], axis=0), (8, 128))
    place = dot_place()
    bb, bh, hh, bg, hg = (
        jnp.sum(jnp.where(place == i, dots, 0.0), axis=1, keepdims=True) for i in range(5)
    )
    ratio = bh / bb
    alpha = bb / (shift * bb + bh)
    rest = hh - ratio * bh
    beta = alpha * alpha * rest / bb
    curve = shift * rest + ratio * (ratio * bh - hh) - ratio * bg + hg
    cross = (ratio * bh - hh) + (ratio * (shift * bb + bh) - shift * bh - bg)
    curving = alpha * alpha * curve + alpha * beta * cross + beta * beta * (shift * bb + bh)
    step = alpha * alpha * rest / curving
    gain = alpha * ratio + beta
    b, h, g = field[...], first[...], second[...]
    direction = gain * b - alpha * h
    residue = alpha * (ratio * b - h)
    image = gain * (shift * b + h) - alpha * (shift * h + g)
    solved[...] = alpha * b + step * direction
    residual[...] = residue - step * image


def on_device(
    points,
    right_side,
    near_list,
    near_count,
    leaf_skeleton_basis,
    leaf_transfer,
    pair_transfer,
    group_transfer,
    pair_coupling,
    group_coupling,
    top_coupling,
    pair_far,
    group_far,
    top_far,
):
    leaves = near_list.shape[0]
    device = lax.axis_index(BOTH)
    total = lax.axis_size(BOTH)
    side = device % 2
    node = device // 2
    top_id = lax.axis_index("leaf") // 4
    rank = leaf_skeleton_basis.shape[1]

    swap_in = [(i, i ^ 1) for i in range(total)]
    swap_out = [(i, i + 1) for i in range(1, total - 1, 2)]
    swap_out += [(j, i) for i, j in swap_out]
    inside = lambda value: lax.ppermute(value, BOTH, swap_in)
    outside = lambda value: lax.ppermute(value, BOTH, swap_out)

    ints = jnp.concatenate(
        [
            side.reshape(1),
            lax.dynamic_index_in_dim(pair_far, node, 0, keepdims=False),
            group_far[0],
            lax.dynamic_index_in_dim(top_far, top_id, 0, keepdims=False),
            top_id.reshape(1),
        ]
    ).astype(jnp.int32)

    holder = near_list // leaves
    used = jnp.arange(NEAR, dtype=jnp.int32)[None, :] < near_count[:, None]
    target = jnp.broadcast_to(jnp.arange(leaves, dtype=jnp.int32)[:, None], near_list.shape)
    window = jnp.where(holder == device, 0, jnp.where(holder == (device ^ 1), leaves, 2 * leaves))
    count, pairs = pair_list(used, 64 * target + window + near_list % leaves, 64 * leaves)

    def exchange(partial):
        mine = cluster_call(
            cluster_kernel, (lax.axis_size("clus"), 8, 3 * rank // 2),
            ints, partial, inside(partial), pair_transfer[0], name="cluster",
        )
        shares = lax.all_to_all(mine, "clus", 0, 0, tiled=True)
        block = cluster_call(
            group_kernel, (lax.axis_size("leaf"), shares.shape[0] // 2 + 2, 8, rank),
            shares, group_transfer[0], name="group",
        )
        fields = lax.all_to_all(block, "leaf", 0, 0, tiled=True)
        return cluster_call(
            coarse_kernel, (8, rank // 2), ints, fields.reshape(-1, 8, rank), pair_transfer[0],
            group_transfer[0], pair_coupling[0], group_coupling[0], name="coarse",
            scratch=[pltpu.VMEM(top_coupling.shape[1:], f32), pltpu.SemaphoreType.DMA],
            far_away=[top_coupling],
        )

    halo, decay = first_halo(points, right_side)
    halos = (halo, inside(halo), outside(halo))
    upward = far_up(right_side, leaf_skeleton_basis, leaf_transfer)
    down = exchange(upward)
    near = near_field(count, pairs, points, right_side, decay, halos, halos)
    first, upward, dots = far_down_up(
        ints, down, inside(down), near, right_side, leaf_skeleton_basis, leaf_transfer
    )
    sources = next_halo(first, decay, halo)
    sources = (sources, inside(sources), outside(sources))
    down = exchange(upward)
    near = near_field(count, pairs, points, first, decay, halos, sources)
    second, dots = far_down(
        ints, down, inside(down), near, right_side, first, dots, leaf_skeleton_basis,
        leaf_transfer, total,
    )
    sums = lax.all_to_all(dots, BOTH, 0, 0, tiled=True)
    return pl.pallas_call(
        last_kernel,
        out_shape=[jax.ShapeDtypeStruct(right_side.shape, f32)] * 2,
        in_specs=[VMEM] * 4,
        out_specs=[VMEM] * 2,
        compiler_params=params(),
        name="last",
    )(sums, right_side, first, second)


def solution(mesh):
    in_specs = (
        P(None, BOTH),
        P(None, BOTH),
        P(BOTH, None),
        P(BOTH),
        P(BOTH, None, None),
        P(BOTH, None, None),
        P(BOTH, None, None),
        P("leaf", None, None),
        P(BOTH, None, None, None),
        P("leaf", None, None, None),
        P(),
        P(),
        P("leaf", None),
        P(),
    )
    out_specs = (P(None, BOTH), P(None, BOTH))
    return jax.shard_map(
        on_device, mesh=mesh, in_specs=in_specs, out_specs=out_specs, check_vma=False
    )
```

time: 219 us -> 178 us (0.81); the launches traced: 217 us -> 181 us
  blocking collectives: 96.9 us -> 32.2 us
  waiting for transfers between devices: 0.03 us -> 26 us
  starting transfers between devices: 29.8 us -> 44.3 us
  Pallas kernels: 74.4 us -> 65.4 us
    all_gather x4 -> x0, blocking collectives: 69.2 us -> none  [the longest x2 40.7 us: exchange(): fields = lax.all_gather(block, 'leaf', axis=0, tiled=True)]
    all_to_all x0 -> x3, waiting for transfers between devices: none -> 24.4 us  [the longest x2 19.6 us: exchange(): fields = lax.all_to_all(block, 'leaf', 0, 0, tiled=True)]
    all_to_all x0 -> x3, starting transfers between devices: none -> 16.4 us  [the longest x2 12.2 us: exchange(): fields = lax.all_to_all(block, 'leaf', 0, 0, tiled=True)]
    pallas_call x7 -> x4, Pallas kernels: 49.9 us -> 35.8 us  [the longest x2 31.6 us: near_field(): pl.pallas_call(near_kernel, out_shape=jax.ShapeDtypeStruct(field.shape, f...]
    all_to_all x1 -> x2, blocking collectives: 27.7 us -> 32.2 us  [the longest x1 24.5 us: on_device(): sums = lax.all_to_all(dots, BOTH, 0, 0, tiled=True)]
    pallas_call x6, Pallas kernels: 4.15 us -> 7.96 us  [cluster_call(): pl.pallas_call(kernel, out_shape=jax.ShapeDtypeStruct(shape, f32), in_spe...]
    ppermute x3 -> x2, starting transfers between devices: 7.46 us -> 5.29 us  [on_device(): outside = lambda value: lax.ppermute(value, BOTH, swap_out)]
    ppermute x7 -> x6, starting transfers between devices: 22.3 us -> 22.6 us  [on_device(): inside = lambda value: lax.ppermute(value, BOTH, swap_in)]
  transfers between devices with their start and end apart: 10 -> 11, of which waited for: 0 -> 5; matrix products, arithmetic and copies ran while one was open for 2% -> 1% of each run, Pallas kernels for 27% -> 26%
where the time goes in v1:
time: 178 us; the launch traced here: 181 us
  Pallas kernels  65.4 us (37%)
  starting transfers between devices  44.3 us (25%)
  blocking collectives  32.2 us (18%)
  waiting for transfers between devices  26 us (15%)
  local copies, waits for them, and re-layouts  10.4 us (6%)
    pallas_call x2, Pallas kernels, near_field(): pl.pallas_call(near_kernel, out_shape=jax.ShapeDtypeStruct(field.shape, f...  31.6 us
    all_to_all x1, blocking collectives, on_device(): sums = lax.all_to_all(dots, BOTH, 0, 0, tiled=True)  24.5 us
    ppermute x6, starting transfers between devices, on_device(): inside = lambda value: lax.ppermute(value, BOTH, swap_in)  22.6 us
    all_to_all x2, waiting for transfers between devices, exchange(): fields = lax.all_to_all(block, 'leaf', 0, 0, tiled=True)  19.6 us
    all_to_all x2, starting transfers between devices, exchange(): fields = lax.all_to_all(block, 'leaf', 0, 0, tiled=True)  12.2 us
    unnamed x44, local copies, waits for them, and re-layouts  9.76 us
    pallas_call x1, Pallas kernels, far_down_up(): pl.pallas_call(down_up_kernel, out_shape=[jax.ShapeDtypeStruct(near.shape...  8.03 us
    pallas_call x6, Pallas kernels, cluster_call(): pl.pallas_call(kernel, out_shape=jax.ShapeDtypeStruct(shape, f32), in_spe...  7.96 us
  transfers between devices with their start and end apart: 11, of which 5 were waited for; matrix products, arithmetic and copies ran while one was open for 1% of the time, Pallas kernels for 26%

profile of v1, /device:TPU:1, one launch (start us, length us, event | category | flops | bytes accessed | tf_op | source)
XLA Modules:
  0.0 180.5 jit_solution(10074722723204217828)
XLA Ops:
  1.6 1.2 copy-done.13
  2.8 1.8 first_halo.1
  4.6 1.4 collective-permute-start.2
  6.1 3.2 %collective-permute-start.3 = (bf16[5376,128]{1,0:T(8,128)(2,1)}, bf16[5376,128]{1,0:T(8,128)(2,1)}, u32[]{:S(2)}, u32[]{:S(2)}) collective-permute-start(bf16[5376,128]{1,0:T(8,128)(2,1)} %get-tuple-element.10.own_points.own_sources.packed), channel_id=1, source_target_pairs={{1,2},{3,4},{5,6},{7,8},{9,10},{11,12},{13,14},{15,16},{17,18},{19... | collective-permute-start | bytes 4128776 | tf_op jit(solution)/shard_map/ppermute | solution.py:506
  9.3 2.2 %copy-done.1 = f32[16,256,256]{2,1,0:T(8,128)S(1)} copy-done((f32[16,256,256]{2,1,0:T(8,128)S(1)}, f32[16,256,256]{2,1,0:T(8,128)}, u32[]{:S(2)}) %copy-start.1) | copy-done | bytes 4194328
  11.5 0.9 copy-done.7
  12.4 6.4 %far_up.1.own = f32[8,256]{1,0:T(8,128)S(1)} custom-call(f32[8,8192]{1,0:T(8,128)S(1)} %copy-done.7, f32[16,256,512]{2,1,0:T(8,128)} %basis.5, f32[16,256,256]{2,1,0:T(8,128)S(1)} %copy-done.1), custom_call_target="tpu_custom_call" | custom-call | tf_op jit(solution)/shard_map/far_up/pallas_call | solution.py:275
  20.1 1.3 cluster.2
  21.4 4.2 %all-to-all-start = ((f32[8,8,384]{2,1,0:T(8,128)}), f32[8,8,384]{2,1,0:T(8,128)S(1)}, u32[]{:S(2)}, u32[]{:S(2)}) async-start(f32[8,8,384]{2,1,0:T(8,128)} %cluster.2), calls=%async_computation | async-start | bytes 196608 | tf_op jit(solution)/shard_map/all_to_all | solution.py:529
  25.8 4.8 %all-to-all-done.shares = f32[8,8,384]{2,1,0:T(8,128)S(1)} async-done(((f32[8,8,384]{2,1,0:T(8,128)}), f32[8,8,384]{2,1,0:T(8,128)S(1)}, u32[]{:S(2)}, u32[]{:S(2)}) %all-to-all-start) | async-done | bytes 98336 | tf_op jit(solution)/shard_map/all_to_all | solution.py:529
  30.6 1.1 group.2
  31.7 8.6 %all-to-all-start.1 = ((f32[16,6,8,256]{3,2,1,0:T(8,128)}), f32[16,6,8,256]{3,2,1,0:T(8,128)S(1)}, u32[]{:S(2)}, u32[]{:S(2)}) async-start(f32[16,6,8,256]{3,2,1,0:T(8,128)} %group.2), calls=%async_computation.1 | async-start | bytes 1572864 | tf_op jit(solution)/shard_map/all_to_all | solution.py:534
  41.7 11.6 %all-to-all-done.1 = f32[16,6,8,256]{3,2,1,0:T(8,128)S(1)} async-done(((f32[16,6,8,256]{3,2,1,0:T(8,128)}), f32[16,6,8,256]{3,2,1,0:T(8,128)S(1)}, u32[]{:S(2)}, u32[]{:S(2)}) %all-to-all-start.1) | async-done | bytes 786464 | tf_op jit(solution)/shard_map/all_to_all | solution.py:534
  53.4 2.2 %copy-done.4 = f32[4,4,256,256]{3,2,1,0:T(8,128)S(1)} copy-done((f32[4,4,256,256]{3,2,1,0:T(8,128)S(1)}, f32[4,4,256,256]{3,2,1,0:T(8,128)}, u32[]{:S(2)}) %copy-start.4) | copy-done | bytes 4194328
  55.5 1.9 %coarse.2.own = f32[8,128]{1,0:T(8,128)S(1)} custom-call(s32[14]{0:T(128)S(1)} %concatenate.3.ints, f32[96,8,256]{2,1,0:T(8,128)S(1)} %bitcast.18, f32[128,256]{1,0:T(8,128)S(1)} %bitcast.23, f32[256,256]{1,0:T(8,128)S(1)} %bitcast.15, f32[4,256,128]{2,1,0:T(8,128)S(1)} %bitcast.20, f32[4,256,256]{2,1,0:T(8,128)S(1)} %bitcast.12, ...), custom_call_target="tpu_custom_call" | custom-call | tf_op jit(solution)/shard_map/coarse/pallas_call | solution.py:443
  57.5 2.5 %collective-permute-start.1 = (f32[8,128]{1,0:T(8,128)S(1)}, f32[8,128]{1,0:T(8,128)S(1)}, u32[]{:S(2)}, u32[]{:S(2)}) collective-permute-start(f32[8,128]{1,0:T(8,128)S(1)} %coarse.2.own), channel_id=1, source_target_pairs={{0,1},{1,0},{2,3},{3,2},{4,5},{5,4},{6,7},{7,6},{8,9},{9,8},{10,11... | collective-permute-start | bytes 12296 | tf_op jit(solution)/shard_map/ppermute | solution.py:505
  60.0 15.9 %near_field.2.near = f32[8,8192]{1,0:T(8,128)S(1)} custom-call(s32[1]{0:T(128)} %bitcast.9.count, s32[128]{0:T(128)S(1)} %broadcast_add_fusion.pairs, bf16[64,8192]{1,0:T(8,128)(2,1)S(1)} %copy-done.14, f32[8,8192]{1,0:T(8,128)S(1)} %copy-done.8, f32[8,8192]{1,0:T(8,128)S(1)} %get-tuple-element.9.decay, ...), custom_call_target="tpu_custom_call" | custom-call | flops 23622320128 | bytes 8388608 | tf_op jit(solution)/shard_map/near_field/pallas_call | solution.py:221
  75.8 8.0 %far_down_up.1 = (f32[8,8192]{1,0:T(8,128)S(1)}, f32[8,256]{1,0:T(8,128)S(1)}, f32[3,8,512]{2,1,0:T(8,128)S(1)}) custom-call(s32[14]{0:T(128)S(1)} %concatenate.3.ints, f32[8,128]{1,0:T(8,128)S(1)} %coarse.2.own, f32[8,128]{1,0:T(8,128)S(1)} %collective-permute-done.1.peer, f32[8,8192]{1,0:T(8,128)S(1)} %near_field.2.near, f32[8,8192]{1,0:T(8,128)S(1)} %copy-done.8, ...), custom_call_target="tpu_custom_call" | custom-call | tf_op jit(solution)/shard_map/far_down_up/pallas_call | solution.py:317
  83.9 11.9 %collective-permute-start.4 = (f32[8,256]{1,0:T(8,128)S(1)}, f32[8,256]{1,0:T(8,128)S(1)}, u32[]{:S(2)}, u32[]{:S(2)}) collective-permute-start(f32[8,256]{1,0:T(8,128)S(1)} %get-tuple-element.11.own), channel_id=1, source_target_pairs={{0,1},{1,0},{2,3},{3,2},{4,5},{5,4},{6,7},{7,6},{8,9},{9,8},{10,11... | collective-permute-start | bytes 24584 | tf_op jit(solution)/shard_map/ppermute | solution.py:505
  97.3 7.7 %all_to_all.25.shares = f32[8,8,384]{2,1,0:T(8,128)S(1)} all-to-all(f32[8,8,384]{2,1,0:T(8,128)S(1)} %cluster.3), channel_id=1, replica_groups=mesh['leaf'=16,'clus'=8] {'clus'}, dimensions={0} | all-to-all | bytes 196608 | tf_op jit(solution)/shard_map/all_to_all | solution.py:529
  105.0 1.1 group.3
  106.1 3.6 %all-to-all-start.3 = ((f32[16,6,8,256]{3,2,1,0:T(8,128)}), f32[16,6,8,256]{3,2,1,0:T(8,128)S(1)}, u32[]{:S(2)}, u32[]{:S(2)}) async-start(f32[16,6,8,256]{3,2,1,0:T(8,128)} %group.3), calls=%async_computation.3 | async-start | bytes 1572864 | tf_op jit(solution)/shard_map/all_to_all | solution.py:534
  109.7 2.4 %next_halo.1.own_sources = bf16[1280,128]{1,0:T(8,128)(2,1)} custom-call(f32[8,8192]{1,0:T(8,128)S(1)} %get-tuple-element.12.field.first, f32[8,8192]{1,0:T(8,128)S(1)} %get-tuple-element.9.decay, bf16[5376,128]{1,0:T(8,128)(2,1)} %get-tuple-element.10.own_points.own_sources.packed), custom_call_target="tpu_custom_call" | custom-call | tf_op jit(solution)/shard_map/next_halo/pallas_call | solution.py:123
  113.0 2.1 %collective-permute-start.7 = (bf16[1280,128]{1,0:T(8,128)(2,1)}, bf16[1280,128]{1,0:T(8,128)(2,1)}, u32[]{:S(2)}, u32[]{:S(2)}) collective-permute-start(bf16[1280,128]{1,0:T(8,128)(2,1)} %next_halo.1.own_sources), channel_id=1, source_target_pairs={{1,2},{3,4},{5,6},{7,8},{9,10},{11,12},{13,14},{15,16},{17,18},{19... | collective-permute-start | bytes 983048 | tf_op jit(solution)/shard_map/ppermute | solution.py:506
  115.1 7.9 %all-to-all-done.3 = f32[16,6,8,256]{3,2,1,0:T(8,128)S(1)} async-done(((f32[16,6,8,256]{3,2,1,0:T(8,128)}), f32[16,6,8,256]{3,2,1,0:T(8,128)S(1)}, u32[]{:S(2)}, u32[]{:S(2)}) %all-to-all-start.3) | async-done | bytes 786464 | tf_op jit(solution)/shard_map/all_to_all | solution.py:534
  123.0 2.2 %copy-done.5 = f32[4,4,256,256]{3,2,1,0:T(8,128)S(1)} copy-done((f32[4,4,256,256]{3,2,1,0:T(8,128)S(1)}, f32[4,4,256,256]{3,2,1,0:T(8,128)}, u32[]{:S(2)}) %copy-start.5) | copy-done | bytes 4194328
  125.2 1.9 %coarse.3.own = f32[8,128]{1,0:T(8,128)S(1)} custom-call(s32[14]{0:T(128)S(1)} %concatenate.3.ints, f32[96,8,256]{2,1,0:T(8,128)S(1)} %bitcast.19, f32[128,256]{1,0:T(8,128)S(1)} %bitcast.25, f32[256,256]{1,0:T(8,128)S(1)} %bitcast.17, f32[4,256,128]{2,1,0:T(8,128)S(1)} %bitcast.21, f32[4,256,256]{2,1,0:T(8,128)S(1)} %bitcast.13, ...), custom_call_target="tpu_custom_call" | custom-call | tf_op jit(solution)/shard_map/coarse/pallas_call | solution.py:443
  127.2 5.9 %collective-permute-start.5 = (f32[8,128]{1,0:T(8,128)S(1)}, f32[8,128]{1,0:T(8,128)S(1)}, u32[]{:S(2)}, u32[]{:S(2)}) collective-permute-start(f32[8,128]{1,0:T(8,128)S(1)} %coarse.3.own), channel_id=1, source_target_pairs={{0,1},{1,0},{2,3},{3,2},{4,5},{5,4},{6,7},{7,6},{8,9},{9,8},{10,11... | collective-permute-start | bytes 12296 | tf_op jit(solution)/shard_map/ppermute | solution.py:505
  133.1 15.7 %near_field.3.near = f32[8,8192]{1,0:T(8,128)S(1)} custom-call(s32[1]{0:T(128)} %bitcast.9.count, s32[128]{0:T(128)S(1)} %broadcast_add_fusion.pairs, bf16[64,8192]{1,0:T(8,128)(2,1)S(1)} %copy-done.15, f32[8,8192]{1,0:T(8,128)S(1)} %get-tuple-element.12.field.first, f32[8,8192]{1,0:T(8,128)S(1)} %get-tuple-element.9.decay, ...), custom_call_target="tpu_custom_call" | custom-call | flops 23622320128 | bytes 8388608 | tf_op jit(solution)/shard_map/near_field/pallas_call | solution.py:221
  148.8 6.0 %far_down.1 = (f32[8,8192]{1,0:T(8,128)S(1)}, f32[128,1,128]{2,1,0:T(1,128)S(1)}) custom-call(s32[14]{0:T(128)S(1)} %concatenate.3.ints, f32[8,128]{1,0:T(8,128)S(1)} %coarse.3.own, f32[8,128]{1,0:T(8,128)S(1)} %collective-permute-done.5.peer, f32[8,8192]{1,0:T(8,128)S(1)} %near_field.3.near, f32[8,8192]{1,0:T(8,128)S(1)} %copy-done.8, ...), custom_call_target="tpu_custom_call" | custom-call | tf_op jit(solution)/shard_map/far_down/pallas_call | solution.py:373
  154.8 24.5 %all_to_all.26.sums = f32[128,1,128]{2,1,0:T(1,128)S(1)} all-to-all(f32[128,1,128]{2,1,0:T(1,128)S(1)} %get-tuple-element.14), channel_id=1, replica_groups=mesh['leaf'=16,'clus'=8] {'leaf','clus'}, dimensions={0} | all-to-all | bytes 131072 | tf_op jit(solution)/shard_map/all_to_all | solution.py:558
  179.3 1.2 last.1
  (65 shorter events, 6.0 us)
Async XLA Ops:
  0.6 18.4 %copy-start = (s32[4,4]{1,0:T(4,128)S(1)}, s32[4,4]{1,0:T(4,128)}, u32[]{:S(2)}) copy-start(s32[4,4]{1,0:T(4,128)} %param.27) | copy-start | bytes 196
  0.6 1.0 copy-start.6
  1.6 1.2 copy-start.13
  4.6 14.6 %copy-start.20 = (s32[1,4]{1,0:T(1,128)S(1)}, s32[1,4]{1,0:T(1,128)}, u32[]{:S(2)}) copy-start(s32[1,4]{1,0:T(1,128)} %param.26) | copy-start | bytes 52
  4.6 35.7 %copy-start.21 = (s32[16]{0:T(128)S(1)}, s32[16]{0:T(128)}, u32[]{:S(2)}) copy-start(s32[16]{0:T(128)} %param.17) | copy-start | bytes 196
  4.6 55.3 %collective-permute-start.2 = (bf16[5376,128]{1,0:T(8,128)(2,1)}, bf16[5376,128]{1,0:T(8,128)(2,1)}, u32[]{:S(2)}, u32[]{:S(2)}) collective-permute-start(bf16[5376,128]{1,0:T(8,128)(2,1)} %get-tuple-element.10.own_points.own_sources.packed), channel_id=1, source_target_pairs={{0,1},{1,0},{2,3},{3,2},{4,5},{5,4},{6,7},{7,6},{8,9},{9,8},{10,11... | collective-permute-start | bytes 4128776 | tf_op jit(solution)/shard_map/ppermute | solution.py:505
  6.1 53.9 %collective-permute-start.3 = (bf16[5376,128]{1,0:T(8,128)(2,1)}, bf16[5376,128]{1,0:T(8,128)(2,1)}, u32[]{:S(2)}, u32[]{:S(2)}) collective-permute-start(bf16[5376,128]{1,0:T(8,128)(2,1)} %get-tuple-element.10.own_points.own_sources.packed), channel_id=1, source_target_pairs={{1,2},{3,4},{5,6},{7,8},{9,10},{11,12},{13,14},{15,16},{17,18},{19... | collective-permute-start | bytes 4128776 | tf_op jit(solution)/shard_map/ppermute | solution.py:506
  9.3 2.2 %copy-start.1 = (f32[16,256,256]{2,1,0:T(8,128)S(1)}, f32[16,256,256]{2,1,0:T(8,128)}, u32[]{:S(2)}) copy-start(f32[16,256,256]{2,1,0:T(8,128)} %transfer.5) | copy-start | bytes 12582916
  12.4 6.6 %copy-start.19 = (s32[64,4]{0,1:T(4,128)S(1)}, s32[64,4]{0,1:T(4,128)}, u32[]{:S(2)}) copy-start(s32[64,4]{0,1:T(4,128)} %param.25) | copy-start | bytes 3076
  12.4 7.7 %copy-start.12 = (f32[1,128,256]{2,1,0:T(8,128)S(1)}, f32[1,128,256]{2,1,0:T(8,128)}, u32[]{:S(2)}) copy-start(f32[1,128,256]{2,1,0:T(8,128)} %param.20) | copy-start | bytes 393220
  12.4 13.2 %copy-start.18 = (s32[16,8]{0,1:T(8,128)S(1)}, s32[16,8]{0,1:T(8,128)}, u32[]{:S(2)}) copy-start(s32[16,8]{0,1:T(8,128)} %param.16) | copy-start | bytes 1540
  12.4 18.2 %copy-start.10 = (f32[1,256,256]{2,1,0:T(8,128)S(1)}, f32[1,256,256]{2,1,0:T(8,128)}, u32[]{:S(2)}) copy-start(f32[1,256,256]{2,1,0:T(8,128)} %param.21) | copy-start | bytes 786436
  12.4 40.9 %copy-start.11 = (f32[1,4,256,128]{3,2,1,0:T(8,128)S(1)}, f32[1,4,256,128]{3,2,1,0:T(8,128)}, u32[]{:S(2)}) copy-start(f32[1,4,256,128]{3,2,1,0:T(8,128)} %param.22) | copy-start | bytes 1572868
  18.9 34.5 %copy-start.9 = (f32[1,4,256,256]{3,2,1,0:T(8,128)S(1)}, f32[1,4,256,256]{3,2,1,0:T(8,128)}, u32[]{:S(2)}) copy-start(f32[1,4,256,256]{3,2,1,0:T(8,128)} %param.23) | copy-start | bytes 3145732
  18.9 1.2 collective-permute-start
  21.4 9.2 %all-to-all-start = ((f32[8,8,384]{2,1,0:T(8,128)}), f32[8,8,384]{2,1,0:T(8,128)S(1)}, u32[]{:S(2)}, u32[]{:S(2)}) async-start(f32[8,8,384]{2,1,0:T(8,128)} %cluster.2), calls=%async_computation | async-start | bytes 196608 | tf_op jit(solution)/shard_map/all_to_all | solution.py:529
  31.7 28.2 %copy-start.8 = (f32[8,8192]{1,0:T(8,128)S(1)}, f32[8,8192]{1,0:T(8,128)}, u32[]{:S(2)}) copy-start(f32[8,8192]{1,0:T(8,128)} %field.11) | copy-start | bytes 786436
  31.7 21.7 %all-to-all-start.1 = ((f32[16,6,8,256]{3,2,1,0:T(8,128)}), f32[16,6,8,256]{3,2,1,0:T(8,128)S(1)}, u32[]{:S(2)}, u32[]{:S(2)}) async-start(f32[16,6,8,256]{3,2,1,0:T(8,128)} %group.2), calls=%async_computation.1 | async-start | bytes 1572864 | tf_op jit(solution)/shard_map/all_to_all | solution.py:534
  53.3 2.2 %copy-start.4 = (f32[4,4,256,256]{3,2,1,0:T(8,128)S(1)}, f32[4,4,256,256]{3,2,1,0:T(8,128)}, u32[]{:S(2)}) copy-start(f32[4,4,256,256]{3,2,1,0:T(8,128)} %top_coupling.3) | copy-start | bytes 12582916
  55.5 4.4 %copy-start.14 = (bf16[64,8192]{1,0:T(8,128)(2,1)S(1)}, bf16[64,8192]{1,0:T(8,128)(2,1)}, u32[]{:S(2)}) copy-start(bf16[64,8192]{1,0:T(8,128)(2,1)} %points.5) | copy-start | bytes 3145732
  57.5 18.4 %collective-permute-start.1 = (f32[8,128]{1,0:T(8,128)S(1)}, f32[8,128]{1,0:T(8,128)S(1)}, u32[]{:S(2)}, u32[]{:S(2)}) collective-permute-start(f32[8,128]{1,0:T(8,128)S(1)} %coarse.2.own), channel_id=1, source_target_pairs={{0,1},{1,0},{2,3},{3,2},{4,5},{5,4},{6,7},{7,6},{8,9},{9,8},{10,11... | collective-permute-start | bytes 12296 | tf_op jit(solution)/shard_map/ppermute | solution.py:505
  59.9 15.9 %copy-start.2 = (f32[16,256,256]{2,1,0:T(8,128)S(1)}, f32[16,256,256]{2,1,0:T(8,128)}, u32[]{:S(2)}) copy-start(f32[16,256,256]{2,1,0:T(8,128)} %transfer.5) | copy-start | bytes 12582916
  83.9 21.2 %copy-start.16 = (f32[3,8,512]{2,1,0:T(8,128)}, f32[3,8,512]{2,1,0:T(8,128)S(1)}, u32[]{:S(2)}) copy-start(f32[3,8,512]{2,1,0:T(8,128)S(1)} %get-tuple-element.13.dots_in) | copy-start | bytes 147460
  83.9 12.8 %collective-permute-start.4 = (f32[8,256]{1,0:T(8,128)S(1)}, f32[8,256]{1,0:T(8,128)S(1)}, u32[]{:S(2)}, u32[]{:S(2)}) collective-permute-start(f32[8,256]{1,0:T(8,128)S(1)} %get-tuple-element.11.own), channel_id=1, source_target_pairs={{0,1},{1,0},{2,3},{3,2},{4,5},{5,4},{6,7},{7,6},{8,9},{9,8},{10,11... | collective-permute-start | bytes 24584 | tf_op jit(solution)/shard_map/ppermute | solution.py:505
  106.1 16.9 %all-to-all-start.3 = ((f32[16,6,8,256]{3,2,1,0:T(8,128)}), f32[16,6,8,256]{3,2,1,0:T(8,128)S(1)}, u32[]{:S(2)}, u32[]{:S(2)}) async-start(f32[16,6,8,256]{3,2,1,0:T(8,128)} %group.3), calls=%async_computation.3 | async-start | bytes 1572864 | tf_op jit(solution)/shard_map/all_to_all | solution.py:534
  112.2 20.9 %collective-permute-start.6 = (bf16[1280,128]{1,0:T(8,128)(2,1)}, bf16[1280,128]{1,0:T(8,128)(2,1)}, u32[]{:S(2)}, u32[]{:S(2)}) collective-permute-start(bf16[1280,128]{1,0:T(8,128)(2,1)} %next_halo.1.own_sources), channel_id=1, source_target_pairs={{0,1},{1,0},{2,3},{3,2},{4,5},{5,4},{6,7},{7,6},{8,9},{9,8},{10,11... | collective-permute-start | bytes 983048 | tf_op jit(solution)/shard_map/ppermute | solution.py:505
  113.0 20.1 %collective-permute-start.7 = (bf16[1280,128]{1,0:T(8,128)(2,1)}, bf16[1280,128]{1,0:T(8,128)(2,1)}, u32[]{:S(2)}, u32[]{:S(2)}) collective-permute-start(bf16[1280,128]{1,0:T(8,128)(2,1)} %next_halo.1.own_sources), channel_id=1, source_target_pairs={{1,2},{3,4},{5,6},{7,8},{9,10},{11,12},{13,14},{15,16},{17,18},{19... | collective-permute-start | bytes 983048 | tf_op jit(solution)/shard_map/ppermute | solution.py:506
  123.0 2.2 %copy-start.5 = (f32[4,4,256,256]{3,2,1,0:T(8,128)S(1)}, f32[4,4,256,256]{3,2,1,0:T(8,128)}, u32[]{:S(2)}) copy-start(f32[4,4,256,256]{3,2,1,0:T(8,128)} %top_coupling.3) | copy-start | bytes 12582916
  125.2 7.8 %copy-start.15 = (bf16[64,8192]{1,0:T(8,128)(2,1)S(1)}, bf16[64,8192]{1,0:T(8,128)(2,1)}, u32[]{:S(2)}) copy-start(bf16[64,8192]{1,0:T(8,128)(2,1)} %points.5) | copy-start | bytes 3145732
  127.1 21.6 %copy-start.3 = (f32[16,256,256]{2,1,0:T(8,128)S(1)}, f32[16,256,256]{2,1,0:T(8,128)}, u32[]{:S(2)}) copy-start(f32[16,256,256]{2,1,0:T(8,128)} %transfer.5) | copy-start | bytes 12582916
  127.2 21.6 %copy-start.17 = (f32[3,8,512]{2,1,0:T(8,128)S(1)}, f32[3,8,512]{2,1,0:T(8,128)}, u32[]{:S(2)}) copy-start(f32[3,8,512]{2,1,0:T(8,128)} %copy-done.16) | copy-start | bytes 147460
  127.2 21.6 %collective-permute-start.5 = (f32[8,128]{1,0:T(8,128)S(1)}, f32[8,128]{1,0:T(8,128)S(1)}, u32[]{:S(2)}, u32[]{:S(2)}) collective-permute-start(f32[8,128]{1,0:T(8,128)S(1)} %coarse.3.own), channel_id=1, source_target_pairs={{0,1},{1,0},{2,3},{3,2},{4,5},{5,4},{6,7},{7,6},{8,9},{9,8},{10,11... | collective-permute-start | bytes 12296 | tf_op jit(solution)/shard_map/ppermute | solution.py:505
  (1 other events, 0.9 us)
